TPU v7x, 512 devices: a whole 4x4x16 slice. The times are simulated.
512 devices in a mesh: batch: 16 (over z_hi, y, core), proto: 32 (over z_lo, x).
Axes of the slice: x: 4, y: 4, z: 16 (z_hi: 2, z_lo: 8; z = z_hi * 8 + z_lo), core: 2. Of those that a mesh axis runs over, the one named last changes fastest.
Arguments:
- hidden: bfloat16 [6144, 2048], P('batch', 'proto'), may hold values from -6 to 6
- w_last: bfloat16 [2048, 256], P('proto'), may hold values from -0.125 to 0.125
- student_protos: bfloat16 [256, 131072], P(None, 'proto'), may hold values from -6 to 6
- teacher_bneck: bfloat16 [6144, 256], P('batch'), may hold values from -8 to 8
- teacher_protos: bfloat16 [256, 131072], P(None, 'proto'), may hold values from -8 to 8
Outputs:
- proto_grad: float32 [256, 131072], P('batch', 'proto')
- weight_grad: float32 [2048, 256], P('proto')
All inputs are finite; a program needn't handle non-finite values.
Results may differ from a plain program's by a relative error of at most 0.0029.
The roundings to bfloat16 on the way count: a program that leaves them out, or rounds other values in their place, can miss the bound.
Values may be sent and summed in bfloat16 or wider, within the bound.
A program may use at most 64 MiB of HBM per device.

v0:
```python
import jax
import jax.numpy as jnp
from jax import lax
from jax.sharding import PartitionSpec as P

PROTOS = 131072
ITERS = 3


epsilon = 1e-06


def row_unit(values):
    floats = values.astype(jnp.float32)
    return (floats * lax.rsqrt(jnp.sum(floats * floats, axis=1) + epsilon)[:, None]).astype(
        jnp.bfloat16
    )


def column_unit(values):
    floats = values.astype(jnp.float32)
    scale = lax.rsqrt(jnp.sum(floats * floats, axis=0) + epsilon)
    return (scale, floats * scale[None, :])


def per_device(hidden, w_last, student_protos, teacher_bneck, teacher_protos):
    crop_rows = hidden.shape[0]
    all_crops = crop_rows * lax.axis_size("batch")
    full_hidden, full_weight = (
        lax.all_gather(hidden, "proto", axis=1, tiled=True),
        lax.all_gather(w_last, "proto", axis=0, tiled=True),
    )
    bottleneck = jnp.dot(full_hidden, full_weight, preferred_element_type=jnp.float32)
    row_scale = lax.rsqrt(jnp.sum(bottleneck * bottleneck, axis=1) + epsilon)
    unit_rows = bottleneck * row_scale[:, None]
    student_rows = unit_rows.astype(jnp.bfloat16)
    col_scale, unit_cols = column_unit(student_protos)
    student_cols = unit_cols.astype(jnp.bfloat16)
    teacher_rows = row_unit(teacher_bneck)
    teacher_scale, teacher_float = column_unit(teacher_protos)
    teacher_cols = teacher_float.astype(jnp.bfloat16)
    student_exp = jnp.exp(
        10.0 * jnp.dot(student_rows, student_cols, preferred_element_type=jnp.float32)
    )
    teacher_exp = jnp.exp(
        25.0 * jnp.dot(teacher_rows, teacher_cols, preferred_element_type=jnp.float32)
    )
    student_local = jnp.sum(student_exp, axis=1)
    student_total = lax.psum(student_local, "proto")
    crop_scale = jnp.ones((crop_rows,), jnp.float32)
    proto_scale = jnp.ones((teacher_exp.shape[1],), jnp.float32)
    for sweep in range(ITERS):
        proto_mass = lax.psum(jnp.sum(teacher_exp * crop_scale[:, None], axis=0), "batch")
        proto_scale = 1.0 / (PROTOS * proto_mass)
        crop_local = jnp.sum(teacher_exp * proto_scale[None, :], axis=1)
        crop_mass, student_total = (lax.psum(crop_local, "proto"), student_total)
        crop_scale = 1.0 / (all_crops * crop_mass)
    probs = student_exp / student_total[:, None]
    targets = (all_crops * crop_scale)[:, None] * teacher_exp * proto_scale[None, :]
    logit_grad = ((probs - targets) * (PROTOS / 128 * 10.0)).astype(jnp.bfloat16)
    row_local = lax.dot_general(
        logit_grad, student_cols, (((1,), (1,)), ((), ())), preferred_element_type=jnp.float32
    )
    row_grad = lax.psum(row_local, "proto")
    share_rows = student_rows.shape[1] // lax.axis_size("batch")
    summed = lax.psum_scatter(
        lax.dot_general(
            student_rows, logit_grad, (((0,), (0,)), ((), ())), preferred_element_type=jnp.float32
        ),
        "batch",
        scatter_dimension=0,
        tiled=True,
    )
    own_units = lax.dynamic_slice_in_dim(
        unit_cols, lax.axis_index("batch") * share_rows, share_rows, 0
    )
    column_dot = lax.psum(jnp.sum(own_units * summed, axis=0), "batch")
    proto_grad = col_scale[None, :] * (summed - own_units * column_dot[None, :])
    bottleneck_grad = (
        row_scale[:, None] * (row_grad - unit_rows * jnp.sum(unit_rows * row_grad, axis=1)[:, None])
    ).astype(jnp.bfloat16)
    weight_local = lax.dot_general(
        hidden, bottleneck_grad, (((0,), (0,)), ((), ())), preferred_element_type=jnp.float32
    )
    weight_grad = lax.psum(weight_local, "batch")
    return (proto_grad, weight_grad)


def solution(mesh):
    placed = (
        P("batch", "proto"),
        P("proto", None),
        P(None, "proto"),
        P("batch", None),
        P(None, "proto"),
    )
    return jax.shard_map(
        per_device,
        mesh=mesh,
        in_specs=placed,
        out_specs=(P("batch", "proto"), P("proto", None)),
        check_vma=False,
    )
```

profile of v0, /device:TPU:1, one launch (start us, length us, event | category | flops | bytes accessed | tf_op | source)
XLA Modules:
  0.0 1614.9 jit_solution(6883086152666652408)
XLA Ops:
  8.7 2.0 fusion.1
  11.8 5.9 fusion.15
  17.7 126.6 %psum.71 = f32[4096]{0:T(1024)S(1)} all-reduce(f32[4096]{0:T(1024)S(1)} %get-tuple-element.6), channel_id=1, replica_groups=mesh['batch'=16,'proto'=32] {'batch'}, use_global_device_ids=true, to_apply=%region_7.0 | all-reduce | flops 4096 | bytes 32768 | tf_op jit(solution)/shard_map/psum | solution.py:53
  144.3 3.3 multiply_reduce_fusion.4
  147.7 105.3 %psum.72 = f32[384]{0:T(512)S(1)} all-reduce(f32[384]{0:T(512)S(1)} %multiply_reduce_fusion.4), channel_id=1, replica_groups=mesh['batch'=16,'proto'=32] {'proto'}, use_global_device_ids=true, to_apply=%region_9.0 | all-reduce | flops 384 | bytes 3072 | tf_op jit(solution)/shard_map/psum | solution.py:56
  253.0 3.7 multiply_reduce_fusion.3
  256.6 136.1 %psum.73 = f32[4096]{0:T(1024)S(1)} all-reduce(f32[4096]{0:T(1024)S(1)} %multiply_reduce_fusion.3), channel_id=1, replica_groups=mesh['batch'=16,'proto'=32] {'batch'}, use_global_device_ids=true, to_apply=%region_11.0 | all-reduce | flops 4096 | bytes 32768 | tf_op jit(solution)/shard_map/psum | solution.py:53
  392.7 3.3 multiply_reduce_fusion.2
  396.1 99.4 %psum.74 = f32[384]{0:T(512)S(1)} all-reduce(f32[384]{0:T(512)S(1)} %multiply_reduce_fusion.2), channel_id=1, replica_groups=mesh['batch'=16,'proto'=32] {'proto'}, use_global_device_ids=true, to_apply=%region_13.0 | all-reduce | flops 384 | bytes 3072 | tf_op jit(solution)/shard_map/psum | solution.py:56
  495.5 3.6 multiply_reduce_fusion.1
  499.1 136.1 %psum.75 = f32[4096]{0:T(1024)S(1)} all-reduce(f32[4096]{0:T(1024)S(1)} %multiply_reduce_fusion.1), channel_id=1, replica_groups=mesh['batch'=16,'proto'=32] {'batch'}, use_global_device_ids=true, to_apply=%region_15.0 | all-reduce | flops 4096 | bytes 32768 | tf_op jit(solution)/shard_map/psum | solution.py:53
  635.7 3.3 multiply_reduce_fusion
  639.1 2.5 multiply_reduce_fusion.6
  641.6 4.1 fusion.16
  645.6 100.5 %all-reduce = (f32[384]{0:T(512)S(1)}, f32[384]{0:T(512)S(1)}) all-reduce(f32[384]{0:T(512)S(1)} %multiply_reduce_fusion, f32[384]{0:T(512)S(1)} %get-tuple-element.8), channel_id=1, replica_groups=mesh['batch'=16,'proto'=32] {'proto'}, use_global_device_ids=true, to_apply=%region_17.0 | all-reduce | flops 768 | bytes 6144 | tf_op jit(solution)/shard_map/psum | solution.py:56
  746.1 5.6 multiply_convert_fusion
  753.4 2.1 fusion.5
  755.6 5.1 fusion.14
  760.7 2.5 convert_multiply_fusion.2
  763.2 430.0 %all-reduce.4.cloned.1.call-done = f32[384,256]{0,1:T(8,128)} async-done(((f32[384,256]{0,1:T(8,128)}), f32[384,256]{0,1:T(8,128)}) %all-reduce.4.cloned.1.call-update) | async-done | bytes 393232 | tf_op jit(solution)/shard_map/psum | solution.py:64
  1194.3 1.8 convolution_bitcast_fusion
  1196.2 172.7 %reduce-scatter.2.cloned.1.call-done = f32[16,4096]{1,0:T(8,128)} async-done(((f32[256,4096]{1,0:T(8,128)}), f32[16,4096]{1,0:T(8,128)}) %reduce-scatter.2.cloned.1.call-update) | async-done | bytes 262160 | tf_op jit(solution)/shard_map/reduce_scatter | solution.py:66
  1370.0 111.6 %psum.77 = f32[4096]{0:T(1024)S(1)} all-reduce(f32[4096]{0:T(1024)S(1)} %multiply_reduce_fusion.7), channel_id=1, replica_groups=mesh['batch'=16,'proto'=32] {'batch'}, use_global_device_ids=true, to_apply=%region_20.0 | all-reduce | flops 4096 | bytes 32768 | tf_op jit(solution)/shard_map/psum | solution.py:77
  1483.4 123.5 %all-reduce.6.cloned.1.call-done = f32[64,256]{1,0:T(8,128)} async-done(((f32[64,256]{1,0:T(8,128)}), f32[64,256]{1,0:T(8,128)}) %all-reduce.6.cloned.1.call-update) | async-done | bytes 65552 | tf_op jit(solution)/shard_map/psum | solution.py:85
  (34 shorter events, 10.3 us)
Async XLA Ops:
  7.2 631.9 %all-gather.5.cloned.1.call-start = ((), (), s32[]{:S(2)}) async-start(), calls=%async_computation.2 | async-start | bytes 1081344 | tf_op jit(solution)/shard_map/all_gather | solution.py:31
  7.9 631.2 %all-gather.3.cloned.1.call-start = ((), (), s32[]{:S(2)}) async-start(), calls=%async_computation.1 | async-start | bytes 1622016 | tf_op jit(solution)/shard_map/all_gather | solution.py:30
  8.6 1184.6 %all-reduce.4.cloned.1.call-start = ((), (), s32[]{:S(2)}) async-start(), calls=%async_computation.4 | async-start | bytes 786432 | tf_op jit(solution)/shard_map/psum | solution.py:64
  396.0 239.2 %copy-start = (bf16[256,4096]{1,0:T(8,128)(2,1)S(1)}, bf16[256,4096]{1,0:T(8,128)(2,1)}, u32[]{:S(2)}) copy-start(bf16[256,4096]{1,0:T(8,128)(2,1)} %param.7) | copy-start | bytes 6291460
  751.7 1.7 copy-start.1
  755.5 613.4 %reduce-scatter.2.cloned.1.call-start = ((), (), s32[]{:S(2)}) async-start(), calls=%async_computation.3 | async-start | bytes 4456448 | tf_op jit(solution)/shard_map/reduce_scatter | solution.py:66
  760.7 433.7 %copy-start.2 = (bf16[384,64]{0,1:T(8,128)(2,1)S(1)}, bf16[384,64]{0,1:T(8,128)(2,1)}, u32[]{:S(2)}) copy-start(bf16[384,64]{0,1:T(8,128)(2,1)} %param.5) | copy-start | bytes 147460
  760.7 846.2 %all-reduce.6.cloned.1.call-start = ((), (), s32[]{:S(2)}) async-start(), calls=%async_computation.5 | async-start | bytes 131072 | tf_op jit(solution)/shard_map/psum | solution.py:85
Sparse Core Ops, SparseCore 0:
  10.1 206.6 all-gather.4
  218.8 221.2 all-gather.2
  755.6 437.5 all-reduce.3
  1198.8 170.0 reduce-scatter.1
  1372.2 234.5 all-reduce.5
where the time goes:
time: 1620 us; the launch traced here: 1610 us
  blocking collectives  816 us (50%)
  waiting for transfers between devices  728 us (45%)
  other arithmetic  32.9 us (2%)
  matrix products  21.4 us (1%)
    psum x1, waiting for transfers between devices, per_device(): row_grad = lax.psum(row_local, 'proto')  430 us
    psum x3, blocking collectives, per_device(): lax.psum(jnp.sum(teacher_exp * crop_scale[:, None], axis=0), 'batch')  399 us
    psum x3, blocking collectives, per_device(): crop_mass, student_total = (lax.psum(crop_local, 'proto'), student_total)  305 us
    reduce_scatter x1, waiting for transfers between devices, per_device(): lax.psum_scatter(lax.dot_general(student_rows, logit_grad, (((0,), (0,)),...  173 us
    psum x1, waiting for transfers between devices, per_device(): weight_grad = lax.psum(weight_local, 'batch')  123 us
    psum x1, blocking collectives, per_device(): column_dot = lax.psum(jnp.sum(own_units * summed, axis=0), 'batch')  112 us
  transfers between devices with their start and end apart: 5, of which 3 were waited for; matrix products, arithmetic and copies ran while one was open for 2% of the time, Pallas kernels for 0%

commit v1 on v0

v1 whole, which is shorter than its diff:
```python
import functools

import jax
import jax.numpy as jnp
from jax import lax
from jax.experimental import pallas as pl
from jax.experimental.pallas import tpu as pltpu
from jax.sharding import PartitionSpec as P

PROTOS = 131072
CROPS = 6144
ITERS = 3
EPS = 1e-06
F32 = jnp.float32
BF16 = jnp.bfloat16
MESH = pl.DeviceIdType.MESH

ROWS = 384
COLS = 4096
DIM = 256
CHUNK = 512
NCHUNK = COLS // CHUNK
LANES = 128
NX, NZ, NY = 4, 8, 4
OWN = 16
SHARDS = 6


def ds(start, size):
    return pl.ds(pl.multiple_of(start, size), size)


def kernel(
    hidden, w_last, sp, tb, tp, out_pg, out_wg,
    kexp, sexp, scols, cscale, trows, ub, wide, vrow, acc, sacc, part,
    xrecv, zsrc, zrecv, unit, rscale, srows, rowg, rxrecv, rzsrc, rzrecv, brows,
    nb, fsrc, fb, pm, pmt, colall, crecv, ysend, yrecv, zhsend, zhrecv, total,
    wsrc, wrecv, wfsrc, wfrecv, wfull,
    nb_s, nb_r, fb_s, fb_r, pm_s, pm_r, x_s, x_r, z_s, z_r, az_s, az_r, ax_s, ax_r,
    c_s, c_r, y_s, y_r, zh_s, zh_r, w_s, w_r, wf_s, wf_r, wg_s, wg_r,
):
    b = lax.axis_index("batch")
    p = lax.axis_index("proto")
    zh = b // 8
    k = b % 8
    y = k // 2
    c = b % 2
    z = p // NX
    x = p % NX

    def near(d):
        return {"batch": zh * 8 + (k + d) % 8, "proto": p}

    def far():
        return {"batch": (1 - zh) * 8 + k, "proto": p}

    def core():
        return {"batch": zh * 8 + y * 2 + (1 - c), "proto": p}

    def along_y(d):
        return {"batch": zh * 8 + ((y + d) % NY) * 2 + c, "proto": p}

    def along_x(d):
        return {"batch": b, "proto": z * NX + (x + d) % NX}

    def at_z(j):
        return {"batch": b, "proto": j * NX + x}

    def group(d):
        return {"batch": b, "proto": (p + d) % 32}

    def remote(src, dst, ss, rs, dev):
        return pltpu.make_async_remote_copy(
            src_ref=src, dst_ref=dst, send_sem=ss, recv_sem=rs, device_id=dev, device_id_type=MESH
        )

    def await_bytes(ref, sem):
        pltpu.make_async_copy(ref, ref, sem).wait()

    barrier = pltpu.get_barrier_semaphore()

    def greet(dev):
        pl.semaphore_signal(barrier, inc=1, device_id=dev, device_id_type=MESH)

    for d in range(1, 8):
        greet(near(d))
    greet(far())
    for d in range(1, 32):
        greet(group(d))

    t = tb[...].astype(F32)
    trows[...] = (t * lax.rsqrt(jnp.sum(t * t, axis=1, keepdims=True) + EPS)).astype(BF16)

    def teacher_chunk(i, _):
        cols = ds(i * CHUNK, CHUNK)
        f = tp[:, cols].astype(F32)
        tc = (f * lax.rsqrt(jnp.sum(f * f, axis=0, keepdims=True) + EPS)).astype(BF16)
        e = jnp.exp(25.0 * jnp.dot(trows[...], tc, preferred_element_type=F32))
        kexp[:, cols] = e
        wide[0:1, cols] = jnp.sum(e, axis=0, keepdims=True)
        return 0

    lax.fori_loop(0, NCHUNK, teacher_chunk, 0)
    part[...] = jnp.dot(hidden[...], w_last[...], preferred_element_type=F32)
    pl.semaphore_wait(barrier, 39)

    def pack(s):
        for j in range(32):
            nb[s, k, j : j + 1, :] = wide[0:1, j * LANES : (j + 1) * LANES]

    def near_send(s):
        for d in range(1, 8):
            remote(nb.at[s, k], nb.at[s, k], nb_s.at[s], nb_r.at[s], near(d)).start()

    def near_wait(s):
        await_bytes(nb.at[s, pl.ds(0, 7)], nb_r.at[s])

    def far_send(s):
        fsrc[s] = jnp.sum(nb[s], axis=0)
        remote(fsrc.at[s], fb.at[s], fb_s.at[s], fb_r.at[s], far()).start()

    def far_wait(s):
        remote(fsrc.at[s], fb.at[s], fb_s.at[s], fb_r.at[s], far()).wait()
        await_bytes(nb.at[s, pl.ds(0, 7)], nb_s.at[s])
        return fsrc[s] + fb[s]

    def unpack(v):
        for j in range(32):
            vrow[0:1, j * LANES : (j + 1) * LANES] = v[j : j + 1, :]

    def lanes_of(ref, i):
        blk = ref[i * LANES : (i + 1) * LANES, :]
        return jnp.sum(blk.T, axis=0, keepdims=True)

    def rows_of(v):
        return jnp.broadcast_to(v, (LANES, LANES)).T

    def group_send(buf, s):
        for d in range(1, 32):
            remote(buf.at[p], buf.at[p], pm_s.at[s], pm_r.at[s], group(d)).start()

    def group_wait(buf, s):
        await_bytes(buf.at[pl.ds(0, 31)], pm_r.at[s])
        await_bytes(buf.at[pl.ds(0, 31)], pm_s.at[s])
        return jnp.sum(buf[...], axis=0)

    def row_pass():
        def block(r, _):
            rows = ds(r * 64, 64)

            def step(i, a):
                q = kexp[rows, ds(i * CHUNK, CHUNK)] * vrow[0:1, ds(i * CHUNK, CHUNK)]
                for j in range(CHUNK // LANES):
                    a = a + q[:, j * LANES : (j + 1) * LANES]
                return a

            acc[rows, :] = lax.fori_loop(0, NCHUNK, step, jnp.zeros((64, LANES), F32))
            return 0

        lax.fori_loop(0, ROWS // 64, block, 0)

    def col_pass():
        def step(i, _):
            for j in range(2):
                cols = ds(i * 256 + j * LANES, LANES)
                wide[0:1, cols] = jnp.sum(kexp[:, cols] * ub[...], axis=0, keepdims=True)
            return 0

        lax.fori_loop(0, COLS // 256, step, 0)

    def rs_x_send(s, src, dst):
        for d in range(1, NX):
            rows = ds(((x + d) % NX) * 96, 96)
            remote(src.at[rows], dst.at[d - 1], x_s.at[s], x_r.at[s], along_x(d)).start()

    def rs_z_send(s, src, xr, zs, zr):
        await_bytes(xr, x_r.at[s])
        red = src[ds(x * 96, 96), :] + xr[0] + xr[1] + xr[2]
        zs[...] = red.reshape(SHARDS, OWN, DIM)
        for j in range(SHARDS):
            @pl.when(z != j + 1)
            def _():
                remote(zs.at[j], zr.at[z], z_s.at[s], z_r.at[s], at_z(j + 1)).start()

    owner = jnp.logical_and(z >= 1, z <= SHARDS)

    def rs_z_wait(s, zs, zr):
        await_bytes(zr.at[pl.ds(0, 7)], z_r.at[s])
        zr[z] = zs[z - 1]
        return jnp.sum(zr[...], axis=0)

    def rs_sent(s, xr, zs):
        await_bytes(xr, x_s.at[s])

        @pl.when(owner)
        def _():
            await_bytes(zs.at[pl.ds(0, SHARDS - 1)], z_s.at[s])

        @pl.when(jnp.logical_not(owner))
        def _():
            await_bytes(zs, z_s.at[s])

    def ag_z_send(s, full):
        ref = full.at[x, ds((z - 1) * OWN, OWN)]
        for d in range(1, NZ):
            remote(ref, ref, az_s.at[s], az_r.at[s], at_z((z + d) % NZ)).start()

    def ag_x_send(s, full):
        @pl.when(owner)
        def _():
            await_bytes(full.at[0, pl.ds(0, (SHARDS - 1) * OWN)], az_r.at[s])

        @pl.when(jnp.logical_not(owner))
        def _():
            await_bytes(full.at[0], az_r.at[s])

        for d in range(1, NX):
            remote(full.at[x], full.at[x], ax_s.at[s], ax_r.at[s], along_x(d)).start()

    def ag_wait(s, full):
        await_bytes(full.at[pl.ds(0, 3)], ax_r.at[s])
        await_bytes(full.at[pl.ds(0, 3)], ax_s.at[s])

        @pl.when(owner)
        def _():
            for d in range(1, NZ):
                await_bytes(full.at[0, pl.ds(0, OWN)], az_s.at[s])

        return full[...].reshape(ROWS, DIM)

    pack(0)
    near_send(0)
    rs_x_send(0, part, xrecv)

    def student_cols(i, _):
        cols = ds(i * CHUNK, CHUNK)
        f = sp[:, cols].astype(F32)
        sc = lax.rsqrt(jnp.sum(f * f, axis=0, keepdims=True) + EPS)
        cscale[0:1, cols] = sc
        scols[:, cols] = (f * sc).astype(BF16)
        return 0

    lax.fori_loop(0, NCHUNK, student_cols, 0)
    near_wait(0)
    far_send(0)
    rs_z_send(0, part, xrecv, zsrc, zrecv)
    unpack(1.0 / (PROTOS * far_wait(0)))
    row_pass()
    for i in range(3):
        pm[0, p, 0:1, i * LANES : (i + 1) * LANES] = lanes_of(acc, i)
    group_send(pm.at[0], 0)

    @pl.when(owner)
    def _():
        bott = rs_z_wait(0, zsrc, zrecv)
        sc = lax.rsqrt(jnp.sum(bott * bott, axis=1, keepdims=True) + EPS)
        u = bott * sc
        unit[...] = u
        rscale[...] = jnp.broadcast_to(sc, (OWN, DIM))
        srows[x, ds((z - 1) * OWN, OWN), :] = u.astype(BF16)
        ag_z_send(0, srows)

    def crop_scale(total_):
        return 1.0 / (CROPS * total_)

    def set_u(v):
        for i in range(3):
            ub[i * LANES : (i + 1) * LANES, :] = rows_of(v[:, i * LANES : (i + 1) * LANES])

    set_u(crop_scale(group_wait(pm.at[0], 0)))

    col_pass()
    pack(1)
    near_send(1)
    ag_x_send(0, srows)
    near_wait(1)
    far_send(1)
    sr = ag_wait(0, srows)
    sacc[...] = jnp.zeros_like(sacc)

    def student_chunk(i, _):
        cols = ds(i * CHUNK, CHUNK)
        rows = srows[...].reshape(ROWS, DIM)
        e = jnp.exp(10.0 * jnp.dot(rows, scols[:, cols], preferred_element_type=F32))
        sexp[:, cols] = e
        a = sacc[...]
        for j in range(CHUNK // LANES):
            a = a + e[:, j * LANES : (j + 1) * LANES]
        sacc[...] = a
        return 0

    lax.fori_loop(0, NCHUNK, student_chunk, 0)
    unpack(1.0 / (PROTOS * far_wait(1)))
    row_pass()
    for i in range(3):
        pmt[p, 0:1, i * LANES : (i + 1) * LANES] = lanes_of(acc, i)
        pmt[p, 0:1, ROWS + i * LANES : ROWS + (i + 1) * LANES] = lanes_of(sacc, i)
    group_send(pmt, 1)
    rs_sent(0, xrecv, zsrc)
    both = group_wait(pmt, 1)
    set_u(crop_scale(both[:, :ROWS]))
    gain = PROTOS / 128 * 10.0
    student_scale = gain / both[:, ROWS:]

    col_pass()
    pack(2)
    near_send(2)
    for i in range(3):
        sacc[i * LANES : (i + 1) * LANES, :] = rows_of(student_scale[:, i * LANES : (i + 1) * LANES])
    near_wait(2)
    far_send(2)
    unpack(1.0 / (PROTOS * far_wait(2)))
    row_pass()
    for i in range(3):
        pm[1, p, 0:1, i * LANES : (i + 1) * LANES] = lanes_of(acc, i)
    group_send(pm.at[1], 2)
    rowg[...] = jnp.zeros_like(rowg)
    set_u((gain * CROPS) * crop_scale(group_wait(pm.at[1], 2)))

    def c_copy(i):
        cols = ds(i * CHUNK, CHUNK)
        return remote(
            colall.at[:, 1 - c, :, cols], crecv.at[:, :, cols], c_s.at[i], c_r.at[i], core()
        )

    def y_copy(i, d):
        cols = ds(i * CHUNK, CHUNK)
        return remote(
            ysend.at[(y + d) % NY, :, :, cols], yrecv.at[d - 1, :, :, cols],
            y_s.at[i, d - 1], y_r.at[i, d - 1], along_y(d),
        )

    def zh_copy(i):
        cols = ds(i * CHUNK, CHUNK)
        return remote(zhsend.at[:, cols], zhrecv.at[:, cols], zh_s.at[i], zh_r.at[i], far())

    def y_send(i):
        cols = ds(i * CHUNK, CHUNK)
        c_copy(i).wait()
        for g in range(NY):
            for h in range(2):
                s = colall[h * NY + g, c, :, cols] + crecv[h * NY + g, :, cols]
                crecv[h * NY + g, :, cols] = s
                ysend[g, h, :, cols] = s.astype(BF16)
        for d in range(1, NY):
            y_copy(i, d).start()

    def zh_send(i, _):
        cols = ds(i * CHUNK, CHUNK)
        for d in range(1, NY):
            y_copy(i, d).wait()

        def over_y(h):
            s = crecv[h * NY + y, :, cols]
            for d in range(1, NY):
                s = s + yrecv[d - 1, h, :, cols].astype(F32)
            return s

        total[:, cols] = over_y(zh)
        zhsend[:, cols] = over_y(1 - zh).astype(BF16)
        zh_copy(i).start()
        return 0

    def grad_chunk(i, _):
        cols = ds(i * CHUNK, CHUNK)
        v = vrow[0:1, cols]
        pieces = []
        for j in range(CHUNK // LANES):
            lane = ds(i * CHUNK + j * LANES, LANES)
            vj = v[:, j * LANES : (j + 1) * LANES]
            pieces.append(
                (sexp[:, lane] * sacc[...] - (kexp[:, lane] * vj) * ub[...]).astype(BF16)
            )
        lg = jnp.concatenate(pieces, axis=1)
        rows = srows[...].reshape(ROWS, DIM)
        colg = lax.dot_general(rows, lg, (((0,), (0,)), ((), ())), preferred_element_type=F32)
        colall[:, :, :, cols] = colg.reshape(8, 2, OWN, CHUNK)
        c_copy(i).start()
        rowg[...] += lax.dot_general(
            lg, scols[:, cols], (((1,), (1,)), ((), ())), preferred_element_type=F32
        )
        un = sp[:, cols].astype(F32) * cscale[0:1, cols]
        wide[0:1, cols] = jnp.sum(un * colg, axis=0, keepdims=True)

        @pl.when(i > 0)
        def _():
            y_send(i - 1)

        return 0

    lax.fori_loop(0, NCHUNK, grad_chunk, 0)
    rs_x_send(1, rowg, rxrecv)
    pack(3)
    near_send(3)
    y_send(NCHUNK - 1)
    rs_z_send(1, rowg, rxrecv, rzsrc, rzrecv)
    near_wait(3)
    far_send(3)
    lax.fori_loop(0, 4, zh_send, 0)

    @pl.when(owner)
    def _():
        g = rs_z_wait(1, rzsrc, rzrecv)
        u = unit[...]
        dot = jnp.sum(u * g, axis=1, keepdims=True)
        brows[x, ds((z - 1) * OWN, OWN), :] = (rscale[...] * (g - u * dot)).astype(BF16)
        ag_z_send(1, brows)

    lax.fori_loop(4, NCHUNK, zh_send, 0)
    ag_x_send(1, brows)
    unpack(far_wait(3))
    bg = ag_wait(1, brows)
    wg = lax.dot_general(hidden[...], bg, (((0,), (0,)), ((), ())), preferred_element_type=F32)
    wsrc[...] = wg.reshape(8, 8, DIM)
    for d in range(1, 8):
        remote(wsrc.at[(k + d) % 8], wrecv.at[k], w_s, w_r, near(d)).start()

    def finish(i, _):
        cols = ds(i * CHUNK, CHUNK)
        zh_copy(i).wait()
        s = total[:, cols] + zhrecv[:, cols].astype(F32)
        sc = cscale[0:1, cols]
        un = sp[ds(b * OWN, OWN), cols].astype(F32) * sc
        out_pg[:, cols] = sc * (s - un * vrow[0:1, cols])
        return 0

    await_bytes(wrecv.at[pl.ds(0, 7)], w_r)
    wrecv[k] = wsrc[k]
    wfsrc[...] = jnp.sum(wrecv[...], axis=0)
    wf = remote(wfsrc, wfrecv, wf_s, wf_r, far())
    wf.start()
    lax.fori_loop(0, NCHUNK, finish, 0)
    rs_sent(1, rxrecv, rzsrc)
    await_bytes(wsrc.at[pl.ds(0, 7)], w_s)
    wf.wait()
    wfull[k] = wfsrc[...] + wfrecv[...]
    for d in range(1, 8):
        remote(wfull.at[k], wfull.at[k], wg_s, wg_r, near(d)).start()
    await_bytes(wfull.at[pl.ds(0, 7)], wg_r)
    await_bytes(wfull.at[pl.ds(0, 7)], wg_s)
    out_wg[...] = wfull[...].reshape(64, DIM)


def per_device(hidden, w_last, student_protos, teacher_bneck, teacher_protos):
    vm = pltpu.VMEM
    dma = pltpu.SemaphoreType.DMA
    scratch = [
        vm((ROWS, COLS), F32), vm((ROWS, COLS), F32), vm((DIM, COLS), BF16), vm((8, COLS), F32),
        vm((ROWS, DIM), BF16), vm((ROWS, LANES), F32), vm((8, COLS), F32), vm((8, COLS), F32),
        vm((ROWS, LANES), F32), vm((ROWS, LANES), F32), vm((ROWS, DIM), F32),
        vm((3, 96, DIM), F32), vm((SHARDS, OWN, DIM), F32), vm((NZ, OWN, DIM), F32),
        vm((OWN, DIM), F32), vm((OWN, DIM), F32), vm((NX, 96, DIM), BF16), vm((ROWS, DIM), F32),
        vm((3, 96, DIM), F32), vm((SHARDS, OWN, DIM), F32), vm((NZ, OWN, DIM), F32),
        vm((NX, 96, DIM), BF16),
        vm((4, 8, 32, LANES), F32), vm((4, 32, LANES), F32), vm((4, 32, LANES), F32),
        vm((2, 32, 1, ROWS), F32), vm((32, 1, 2 * ROWS), F32),
        vm((8, 2, OWN, COLS), F32), vm((8, OWN, COLS), F32), vm((NY, 2, OWN, COLS), BF16),
        vm((3, 2, OWN, COLS), BF16), vm((OWN, COLS), BF16), vm((OWN, COLS), BF16),
        vm((OWN, COLS), F32),
        vm((8, 8, DIM), F32), vm((8, 8, DIM), F32), vm((8, DIM), F32), vm((8, DIM), F32),
        vm((8, 8, DIM), F32),
        dma((4,)), dma((4,)), dma((4,)), dma((4,)), dma((3,)), dma((3,)),
        dma((2,)), dma((2,)), dma((2,)), dma((2,)), dma((2,)), dma((2,)), dma((2,)), dma((2,)),
        dma((NCHUNK,)), dma((NCHUNK,)), dma((NCHUNK, 3)), dma((NCHUNK, 3)),
        dma((NCHUNK,)), dma((NCHUNK,)), dma, dma, dma, dma, dma, dma,
    ]
    spec = pl.BlockSpec(memory_space=pltpu.VMEM)
    return pl.pallas_call(
        kernel,
        out_shape=(
            jax.ShapeDtypeStruct((OWN, COLS), F32),
            jax.ShapeDtypeStruct((64, DIM), F32),
        ),
        in_specs=[spec] * 5,
        out_specs=(spec, spec),
        scratch_shapes=scratch,
        compiler_params=pltpu.CompilerParams(
            collective_id=0, has_side_effects=True, vmem_limit_bytes=60 * 1024 * 1024
        ),
        name="dino_head",
    )(hidden, w_last, student_protos, teacher_bneck, teacher_protos)


def solution(mesh):
    placed = (
        P("batch", "proto"),
        P("proto", None),
        P(None, "proto"),
        P("batch", None),
        P(None, "proto"),
    )
    return jax.shard_map(
        per_device,
        mesh=mesh,
        in_specs=placed,
        out_specs=(P("batch", "proto"), P("proto", None)),
        check_vma=False,
    )
```

time: 1620 us -> 147 us (0.09)
  blocking collectives: 816 us -> 0 us
  waiting for transfers between devices: 728 us -> 0 us
  Pallas kernels: 0 us -> 142 us
  other arithmetic: 32.9 us -> 0 us
  matrix products: 21.4 us -> 0 us
    psum x7 -> x0, blocking collectives: 816 us -> none  [the longest x3 399 us: per_device(): lax.psum(jnp.sum(teacher_exp * crop_scale[:, None], axis=0), 'batch')]
    psum x2 -> x0, waiting for transfers between devices: 554 us -> none  [the longest x1 430 us: per_device(): row_grad = lax.psum(row_local, 'proto')]
    reduce_scatter x1 -> x0, waiting for transfers between devices: 173 us -> none  [per_device(): lax.psum_scatter(lax.dot_general(student_rows, logit_grad, (((0,), (0,)),...]
    pallas_call x0 -> x1, Pallas kernels: none -> 142 us  [per_device(): pl.pallas_call(kernel, out_shape=(jax.ShapeDtypeStruct((OWN, COLS), F32),...]
    reduce_sum x10 -> x0, other arithmetic: 23 us -> none  [the longest x3 9.98 us: per_device(): crop_local = jnp.sum(teacher_exp * proto_scale[None, :], axis=1)]
    dot_general x6 -> x0, matrix products: 21.4 us -> none  [the longest x1 5.86 us: per_device(): jnp.dot(teacher_rows, teacher_cols, preferred_element_type=jnp.float32)]
  transfers between devices with their start and end apart: 5 -> 0, of which waited for: 3 -> 0; matrix products, arithmetic and copies ran while one was open for 2% -> 0% of each run, Pallas kernels for 0% -> 0%
where the time goes in v1:
time: 147 us
  Pallas kernels  142 us (97%)
  local copies, waits for them, and re-layouts  4.69 us (3%)
    pallas_call x1, Pallas kernels, per_device(): pl.pallas_call(kernel, out_shape=(jax.ShapeDtypeStruct((OWN, COLS), F32),...  142 us
    unnamed x3, local copies, waits for them, and re-layouts  4.69 us

profile of v1, /device:TPU:1, one launch (start us, length us, event | category | flops | bytes accessed | tf_op | source)
XLA Modules:
  0.0 147.2 jit_solution(13032610406485535583)
XLA Ops:
  0.6 1.5 %copy.7.hidden = bf16[384,64]{1,0:T(8,128)(2,1)} copy(bf16[384,64]{0,1:T(8,128)(2,1)} %param.5) | data formatting | bytes 98304 | tf_op args[0]
  2.2 141.9 %dino_head.1 = (f32[16,4096]{1,0:T(8,128)}, f32[64,256]{1,0:T(8,128)}) custom-call(bf16[384,64]{1,0:T(8,128)(2,1)} %copy.7.hidden, bf16[64,256]{1,0:T(8,128)(2,1)} %w_last.1, bf16[256,4096]{1,0:T(8,128)(2,1)} %sp.1, bf16[384,256]{1,0:T(8,128)(2,1)} %tb.1, bf16[256,4096]{1,0:T(8,128)(2,1)} %tp.1), custom_call_target="tpu_custom_call" | custom-call | tf_op jit(solution)/shard_map/dino_head/pallas_call | solution.py:468
  144.1 1.7 %copy.10 = f32[16,4096]{1,0:T(8,128)} copy(f32[16,4096]{1,0:T(8,128)} %get-tuple-element.4) | data formatting | bytes 524288
  145.8 1.5 copy.11

commit v2 on v1

--- a/solution.py
+++ b/solution.py
@@ -22,6 +22,7 @@
 NCHUNK = COLS // CHUNK
 LANES = 128
 NX, NZ, NY = 4, 8, 4
+ZH0, ZH1 = 0, 4
 OWN = 16
 SHARDS = 6
 
@@ -34,7 +35,7 @@
     hidden, w_last, sp, tb, tp, out_pg, out_wg,
     kexp, sexp, scols, cscale, trows, ub, wide, vrow, acc, sacc, part,
     xrecv, zsrc, zrecv, unit, rscale, srows, rowg, rxrecv, rzsrc, rzrecv, brows,
-    nb, fsrc, fb, pm, pmt, colall, crecv, ysend, yrecv, zhsend, zhrecv, total,
+    nb, fsrc, fb, pm, pmt, lgs, colall, crecv, ysend, yrecv, zhsend, zhrecv, total,
     wsrc, wrecv, wfsrc, wfrecv, wfull,
     nb_s, nb_r, fb_s, fb_r, pm_s, pm_r, x_s, x_r, z_s, z_r, az_s, az_r, ax_s, ax_r,
     c_s, c_r, y_s, y_r, zh_s, zh_r, w_s, w_r, wf_s, wf_r, wg_s, wg_r,
@@ -372,31 +373,38 @@
                 (sexp[:, lane] * sacc[...] - (kexp[:, lane] * vj) * ub[...]).astype(BF16)
             )
         lg = jnp.concatenate(pieces, axis=1)
-        rows = srows[...].reshape(ROWS, DIM)
-        colg = lax.dot_general(rows, lg, (((0,), (0,)), ((), ())), preferred_element_type=F32)
-        colall[:, :, :, cols] = colg.reshape(8, 2, OWN, CHUNK)
-        c_copy(i).start()
+        lgs[:, cols] = lg
         rowg[...] += lax.dot_general(
             lg, scols[:, cols], (((1,), (1,)), ((), ())), preferred_element_type=F32
         )
+        return 0
+
+    def column_chunk(i, _):
+        cols = ds(i * CHUNK, CHUNK)
+        rows = srows[...].reshape(ROWS, DIM)
+        colg = lax.dot_general(
+            rows, lgs[:, cols], (((0,), (0,)), ((), ())), preferred_element_type=F32
+        )
+        colall[:, :, :, cols] = colg.reshape(8, 2, OWN, CHUNK)
+        c_copy(i).start()
         un = sp[:, cols].astype(F32) * cscale[0:1, cols]
         wide[0:1, cols] = jnp.sum(un * colg, axis=0, keepdims=True)
-
-        @pl.when(i > 0)
-        def _():
-            y_send(i - 1)
-
+        return 0
+
+    def y_sends(i, _):
+        y_send(i)
         return 0
 
     lax.fori_loop(0, NCHUNK, grad_chunk, 0)
     rs_x_send(1, rowg, rxrecv)
+    lax.fori_loop(0, NCHUNK, column_chunk, 0)
     pack(3)
     near_send(3)
-    y_send(NCHUNK - 1)
     rs_z_send(1, rowg, rxrecv, rzsrc, rzrecv)
+    lax.fori_loop(0, NCHUNK, y_sends, 0)
     near_wait(3)
     far_send(3)
-    lax.fori_loop(0, 4, zh_send, 0)
+    lax.fori_loop(0, ZH0, zh_send, 0)
 
     @pl.when(owner)
     def _():
@@ -406,8 +414,9 @@
         brows[x, ds((z - 1) * OWN, OWN), :] = (rscale[...] * (g - u * dot)).astype(BF16)
         ag_z_send(1, brows)
 
-    lax.fori_loop(4, NCHUNK, zh_send, 0)
+    lax.fori_loop(ZH0, ZH1, zh_send, 0)
     ag_x_send(1, brows)
+    lax.fori_loop(ZH1, NCHUNK, zh_send, 0)
     unpack(far_wait(3))
     bg = ag_wait(1, brows)
     wg = lax.dot_general(hidden[...], bg, (((0,), (0,)), ((), ())), preferred_element_type=F32)
@@ -454,7 +463,7 @@
         vm((NX, 96, DIM), BF16),
         vm((4, 8, 32, LANES), F32), vm((4, 32, LANES), F32), vm((4, 32, LANES), F32),
         vm((2, 32, 1, ROWS), F32), vm((32, 1, 2 * ROWS), F32),
-        vm((8, 2, OWN, COLS), F32), vm((8, OWN, COLS), F32), vm((NY, 2, OWN, COLS), BF16),
+        vm((ROWS, COLS), BF16), vm((8, 2, OWN, COLS), F32), vm((8, OWN, COLS), F32), vm((NY, 2, OWN, COLS), BF16),
         vm((3, 2, OWN, COLS), BF16), vm((OWN, COLS), BF16), vm((OWN, COLS), BF16),
         vm((OWN, COLS), F32),
         vm((8, 8, DIM), F32), vm((8, 8, DIM), F32), vm((8, DIM), F32), vm((8, DIM), F32),

time: 147 us -> 135 us (0.918)
  Pallas kernels: 142 us -> 130 us
    pallas_call x1, Pallas kernels: 142 us -> 130 us  [per_device(): pl.pallas_call(kernel, out_shape=(jax.ShapeDtypeStruct((OWN, COLS), F32),...]
where the time goes in v2:
time: 135 us
  Pallas kernels  130 us (96%)
  local copies, waits for them, and re-layouts  4.69 us (3%)
    pallas_call x1, Pallas kernels, per_device(): pl.pallas_call(kernel, out_shape=(jax.ShapeDtypeStruct((OWN, COLS), F32),...  130 us
    unnamed x3, local copies, waits for them, and re-layouts  4.69 us

profile of v2, /device:TPU:1, one launch (start us, length us, event | category | flops | bytes accessed | tf_op | source)
XLA Modules:
  0.0 135.0 jit_solution(5975909515211359782)
XLA Ops:
  0.6 1.5 %copy.7.hidden = bf16[384,64]{1,0:T(8,128)(2,1)} copy(bf16[384,64]{0,1:T(8,128)(2,1)} %param.5) | data formatting | bytes 98304 | tf_op args[0]
  2.2 129.7 %dino_head.1 = (f32[16,4096]{1,0:T(8,128)}, f32[64,256]{1,0:T(8,128)}) custom-call(bf16[384,64]{1,0:T(8,128)(2,1)} %copy.7.hidden, bf16[64,256]{1,0:T(8,128)(2,1)} %w_last.1, bf16[256,4096]{1,0:T(8,128)(2,1)} %sp.1, bf16[384,256]{1,0:T(8,128)(2,1)} %tb.1, bf16[256,4096]{1,0:T(8,128)(2,1)} %tp.1), custom_call_target="tpu_custom_call" | custom-call | tf_op jit(solution)/shard_map/dino_head/pallas_call | solution.py:477
  131.9 1.7 %copy.10 = f32[16,4096]{1,0:T(8,128)} copy(f32[16,4096]{1,0:T(8,128)} %get-tuple-element.4) | data formatting | bytes 524288
  133.6 1.5 %copy.11 = f32[64,256]{1,0:T(8,128)} copy(f32[64,256]{1,0:T(8,128)} %get-tuple-element.5) | data formatting | bytes 131072

commit v3 on v2

--- a/solution.py
+++ b/solution.py
@@ -19,7 +19,9 @@
 COLS = 4096
 DIM = 256
 CHUNK = 512
+WIDE = 1024
 NCHUNK = COLS // CHUNK
+HALF = COLS // 2
 LANES = 128
 NX, NZ, NY = 4, 8, 4
 ZH0, ZH1 = 0, 4
@@ -32,12 +34,14 @@
 
 
 def kernel(
-    hidden, w_last, sp, tb, tp, out_pg, out_wg,
+    hidden_in, w_in, sp_in, tb_in, tp_in, out_pg, out_wg,
+    hidden, w_last, sp, tb, tp, in_s, out_s,
     kexp, sexp, scols, cscale, trows, ub, wide, vrow, acc, sacc, part,
     xrecv, zsrc, zrecv, unit, rscale, srows, rowg, rxrecv, rzsrc, rzrecv, brows,
-    nb, fsrc, fb, pm, pmt, lgs, colall, crecv, ysend, yrecv, zhsend, zhrecv, total,
+    nb, fsrc, fb, nbh, vh, xb1, zb1, xb, zb, xbs, zbs, kp, tpr, ubp, accp, lgs, colall, crecv, ysend, yrecv, zhsend, zhrecv, total,
     wsrc, wrecv, wfsrc, wfrecv, wfull,
-    nb_s, nb_r, fb_s, fb_r, pm_s, pm_r, x_s, x_r, z_s, z_r, az_s, az_r, ax_s, ax_r,
+    nb_s, nb_r, fb_s, fb_r, nh_s, nh_r, vh_s, vh_r, xb_s, xb_r, zb_s, zb_r,
+    mi_s, mi_r, tx_s, tx_r, x_s, x_r, z_s, z_r, az_s, az_r, ax_s, ax_r,
     c_s, c_r, y_s, y_r, zh_s, zh_r, w_s, w_r, wf_s, wf_r, wg_s, wg_r,
 ):
     b = lax.axis_index("batch")
@@ -67,8 +71,14 @@
     def at_z(j):
         return {"batch": b, "proto": j * NX + x}
 
-    def group(d):
-        return {"batch": b, "proto": (p + d) % 32}
+    gz = zh * NZ + z
+
+    def ring(d):
+        g = (gz + d) % 16
+        return {"batch": (g // NZ) * 8 + k, "proto": (g % NZ) * NX + x}
+
+    def mirror():
+        return {"batch": (1 - zh) * 8 + k, "proto": (NZ - 1 - z) * NX + x}
 
     def remote(src, dst, ss, rs, dev):
         return pltpu.make_async_remote_copy(
@@ -78,6 +88,20 @@
     def await_bytes(ref, sem):
         pltpu.make_async_copy(ref, ref, sem).wait()
 
+    def load(src, dst, i):
+        return pltpu.make_async_copy(src, dst, in_s.at[i])
+
+    def tp_load(i):
+        cols = ds(i * WIDE, WIDE)
+        return load(tp_in.at[:, cols], tp.at[:, cols], i)
+
+    loads = [load(tb_in, tb, 4), load(hidden_in, hidden, 5), load(w_in, w_last, 6), load(sp_in, sp, 7)]
+    loads[0].start()
+    for i in range(COLS // WIDE):
+        tp_load(i).start()
+    for copy in loads[1:]:
+        copy.start()
+
     barrier = pltpu.get_barrier_semaphore()
 
     def greet(dev):
@@ -85,25 +109,32 @@
 
     for d in range(1, 8):
         greet(near(d))
-    greet(far())
-    for d in range(1, 32):
-        greet(group(d))
-
+    for d in range(1, NX):
+        greet(along_x(d))
+    for d in range(1, 16):
+        greet(ring(d))
+
+    loads[0].wait()
     t = tb[...].astype(F32)
     trows[...] = (t * lax.rsqrt(jnp.sum(t * t, axis=1, keepdims=True) + EPS)).astype(BF16)
 
+    def store_sums(s, i, sums):
+        nb[s, k, ds(i * 8, 8), :] = jnp.concatenate(sums, axis=0)
+
     def teacher_chunk(i, _):
-        cols = ds(i * CHUNK, CHUNK)
+        cols = ds(i * WIDE, WIDE)
+        tp_load(i).wait()
         f = tp[:, cols].astype(F32)
         tc = (f * lax.rsqrt(jnp.sum(f * f, axis=0, keepdims=True) + EPS)).astype(BF16)
         e = jnp.exp(25.0 * jnp.dot(trows[...], tc, preferred_element_type=F32))
+        tp[:, cols] = tc
         kexp[:, cols] = e
-        wide[0:1, cols] = jnp.sum(e, axis=0, keepdims=True)
-        return 0
-
-    lax.fori_loop(0, NCHUNK, teacher_chunk, 0)
-    part[...] = jnp.dot(hidden[...], w_last[...], preferred_element_type=F32)
-    pl.semaphore_wait(barrier, 39)
+        sums = jnp.sum(e, axis=0, keepdims=True)
+        store_sums(0, i, [sums[:, j * LANES : (j + 1) * LANES] for j in range(8)])
+        return 0
+
+    lax.fori_loop(0, COLS // WIDE, teacher_chunk, 0)
+    pl.semaphore_wait(barrier, 25)
 
     def pack(s):
         for j in range(32):
@@ -136,38 +167,80 @@
     def rows_of(v):
         return jnp.broadcast_to(v, (LANES, LANES)).T
 
-    def group_send(buf, s):
-        for d in range(1, 32):
-            remote(buf.at[p], buf.at[p], pm_s.at[s], pm_r.at[s], group(d)).start()
-
-    def group_wait(buf, s):
-        await_bytes(buf.at[pl.ds(0, 31)], pm_r.at[s])
-        await_bytes(buf.at[pl.ds(0, 31)], pm_s.at[s])
+    def x_send(buf, s):
+        for d in range(1, NX):
+            remote(buf.at[x], buf.at[x], xb_s.at[s], xb_r.at[s], along_x(d)).start()
+
+    def x_wait(buf, s):
+        await_bytes(buf.at[pl.ds(0, 3)], xb_r.at[s])
+        await_bytes(buf.at[pl.ds(0, 3)], xb_s.at[s])
         return jnp.sum(buf[...], axis=0)
 
-    def row_pass():
+    def z_send(buf, s, value):
+        buf[gz] = value
+        for d in range(1, 16):
+            remote(buf.at[gz], buf.at[gz], zb_s.at[s], zb_r.at[s], ring(d)).start()
+
+    def z_wait(buf, s):
+        await_bytes(buf.at[pl.ds(0, 15)], zb_r.at[s])
+        await_bytes(buf.at[pl.ds(0, 15)], zb_s.at[s])
+
+    def row_pass(src, dst, col0, v0, chunks):
         def block(r, _):
             rows = ds(r * 64, 64)
 
             def step(i, a):
-                q = kexp[rows, ds(i * CHUNK, CHUNK)] * vrow[0:1, ds(i * CHUNK, CHUNK)]
+                q = src[rows, ds(col0 + i * CHUNK, CHUNK)] * vrow[0:1, ds(v0 + i * CHUNK, CHUNK)]
                 for j in range(CHUNK // LANES):
                     a = a + q[:, j * LANES : (j + 1) * LANES]
                 return a
 
-            acc[rows, :] = lax.fori_loop(0, NCHUNK, step, jnp.zeros((64, LANES), F32))
+            dst[rows, :] = lax.fori_loop(0, chunks, step, jnp.zeros((64, LANES), F32))
             return 0
 
         lax.fori_loop(0, ROWS // 64, block, 0)
 
-    def col_pass():
+    half0 = zh * HALF
+
+    def half_rows(s):
+        row_pass(kexp, acc, half0, half0, HALF // CHUNK)
+        row_pass(kp, accp, 0, half0, HALF // CHUNK)
+        for i in range(3):
+            xb[s, x, zh, 0:1, i * LANES : (i + 1) * LANES] = lanes_of(acc, i)
+            xb[s, x, 1 - zh, 0:1, i * LANES : (i + 1) * LANES] = lanes_of(accp, i)
+
+    def half_cols(s):
         def step(i, _):
-            for j in range(2):
-                cols = ds(i * 256 + j * LANES, LANES)
-                wide[0:1, cols] = jnp.sum(kexp[:, cols] * ub[...], axis=0, keepdims=True)
+            def rows_step(r, sums):
+                for q in range(2):
+                    rows = ds(r * 16 + q * 8, 8)
+                    f = ub[rows, :]
+                    g = ubp[rows, :]
+                    sums = tuple(
+                        sums[j]
+                        + kexp[rows, ds(half0 + i * WIDE + j * LANES, LANES)] * f
+                        + kp[rows, ds(i * WIDE + j * LANES, LANES)] * g
+                        for j in range(8)
+                    )
+                return sums
+
+            zero = jnp.zeros((8, LANES), F32)
+            sums = lax.fori_loop(0, ROWS // 16, rows_step, (zero,) * 8)
+            sums = [jnp.sum(v, axis=0, keepdims=True) for v in sums]
+            nbh[s, k, ds(i * 8, 8), :] = jnp.concatenate(sums, axis=0)
             return 0
 
-        lax.fori_loop(0, COLS // 256, step, 0)
+        lax.fori_loop(0, HALF // WIDE, step, 0)
+        for d in range(1, 8):
+            remote(nbh.at[s, k], nbh.at[s, k], nh_s.at[s], nh_r.at[s], near(d)).start()
+
+    def half_scale(s):
+        await_bytes(nbh.at[s, pl.ds(0, 7)], nh_r.at[s])
+        await_bytes(nbh.at[s, pl.ds(0, 7)], nh_s.at[s])
+        v = 1.0 / (PROTOS * jnp.sum(nbh[s], axis=0))
+        for j in range(16):
+            vrow[0:1, ds(half0 + j * LANES, LANES)] = v[j : j + 1, :]
+        return v
 
     def rs_x_send(s, src, dst):
         for d in range(1, NX):
@@ -229,9 +302,14 @@
 
         return full[...].reshape(ROWS, DIM)
 
-    pack(0)
     near_send(0)
+    loads[1].wait()
+    loads[2].wait()
+    part[...] = lax.dot_general(
+        hidden[...], w_last[...], (((0,), (0,)), ((), ())), preferred_element_type=F32
+    )
     rs_x_send(0, part, xrecv)
+    loads[3].wait()
 
     def student_cols(i, _):
         cols = ds(i * CHUNK, CHUNK)
@@ -244,12 +322,47 @@
     lax.fori_loop(0, NCHUNK, student_cols, 0)
     near_wait(0)
     far_send(0)
+
+    teach = remote(trows.at[ds(x * 96, 96)], tpr.at[x], mi_s, mi_r, mirror())
+    teach.start()
+    unpack(1.0 / (PROTOS * far_wait(0)))
+    row_pass(kexp, acc, 0, 0, NCHUNK)
+    for i in range(3):
+        xb1[x, 0:1, i * LANES : (i + 1) * LANES] = lanes_of(acc, i)
+    x_send(xb1, 0)
+    teach.wait()
+    for d in range(1, NX):
+        remote(tpr.at[x], tpr.at[x], tx_s, tx_r, along_x(d)).start()
+    z_send(zb1, 0, x_wait(xb1, 0))
     rs_z_send(0, part, xrecv, zsrc, zrecv)
-    unpack(1.0 / (PROTOS * far_wait(0)))
-    row_pass()
-    for i in range(3):
-        pm[0, p, 0:1, i * LANES : (i + 1) * LANES] = lanes_of(acc, i)
-    group_send(pm.at[0], 0)
+    await_bytes(tpr.at[pl.ds(0, 3)], tx_r)
+    await_bytes(tpr.at[pl.ds(0, 3)], tx_s)
+
+    def partner_chunk(i, _):
+        cols = ds(half0 + i * WIDE, WIDE)
+        rows = tpr[...].reshape(ROWS, DIM)
+        kp[:, ds(i * WIDE, WIDE)] = jnp.exp(
+            25.0 * jnp.dot(rows, tp[:, cols], preferred_element_type=F32)
+        )
+        return 0
+
+    lax.fori_loop(0, HALF // WIDE, partner_chunk, 0)
+
+    def crop_scale(total_):
+        return 1.0 / (CROPS * total_)
+
+    def set_u(dst, v):
+        for i in range(3):
+            dst[i * LANES : (i + 1) * LANES, :] = rows_of(v[:, i * LANES : (i + 1) * LANES])
+
+    z_wait(zb1, 0)
+    set_u(ub, crop_scale(jnp.sum(zb1[pl.ds(zh * NZ, NZ)], axis=0)))
+    set_u(ubp, crop_scale(jnp.sum(zb1[pl.ds((1 - zh) * NZ, NZ)], axis=0)))
+
+    half_cols(0)
+    half_scale(0)
+    half_rows(0)
+    x_send(xb.at[0], 1)
 
     @pl.when(owner)
     def _():
@@ -261,22 +374,19 @@
         srows[x, ds((z - 1) * OWN, OWN), :] = u.astype(BF16)
         ag_z_send(0, srows)
 
-    def crop_scale(total_):
-        return 1.0 / (CROPS * total_)
-
-    def set_u(v):
-        for i in range(3):
-            ub[i * LANES : (i + 1) * LANES, :] = rows_of(v[:, i * LANES : (i + 1) * LANES])
-
-    set_u(crop_scale(group_wait(pm.at[0], 0)))
-
-    col_pass()
-    pack(1)
-    near_send(1)
+    z_send(zb.at[0], 1, x_wait(xb.at[0], 1))
+    rs_sent(0, xrecv, zsrc)
     ag_x_send(0, srows)
-    near_wait(1)
-    far_send(1)
-    sr = ag_wait(0, srows)
+    z_wait(zb.at[0], 1)
+
+    def of_group(s, g):
+        return crop_scale(jnp.sum(zb[s, :, g], axis=0))
+
+    set_u(ub, of_group(0, zh))
+    set_u(ubp, of_group(0, 1 - zh))
+
+    half_cols(1)
+    ag_wait(0, srows)
     sacc[...] = jnp.zeros_like(sacc)
 
     def student_chunk(i, _):
@@ -291,32 +401,30 @@
         return 0
 
     lax.fori_loop(0, NCHUNK, student_chunk, 0)
-    unpack(1.0 / (PROTOS * far_wait(1)))
-    row_pass()
+    vh[zh] = half_scale(1)
+    v_copy = remote(vh.at[zh], vh.at[zh], vh_s, vh_r, far())
+    v_copy.start()
+    half_rows(1)
+    x_send(xb.at[1], 2)
     for i in range(3):
-        pmt[p, 0:1, i * LANES : (i + 1) * LANES] = lanes_of(acc, i)
-        pmt[p, 0:1, ROWS + i * LANES : ROWS + (i + 1) * LANES] = lanes_of(sacc, i)
-    group_send(pmt, 1)
-    rs_sent(0, xrecv, zsrc)
-    both = group_wait(pmt, 1)
-    set_u(crop_scale(both[:, :ROWS]))
+        xbs[x, 0:1, i * LANES : (i + 1) * LANES] = lanes_of(sacc, i)
+    x_send(xbs, 3)
+    z_send(zb.at[1], 2, x_wait(xb.at[1], 2))
+    zbs[z] = x_wait(xbs, 3)
+    for d in range(1, NZ):
+        remote(zbs.at[z], zbs.at[z], zb_s.at[3], zb_r.at[3], at_z((z + d) % NZ)).start()
+    rowg[...] = jnp.zeros_like(rowg)
+    v_copy.wait()
+    for h in range(2):
+        for j in range(16):
+            at = h * HALF + j * LANES
+            vrow[0:1, at : at + LANES] = vh[h, j : j + 1, :]
     gain = PROTOS / 128 * 10.0
-    student_scale = gain / both[:, ROWS:]
-
-    col_pass()
-    pack(2)
-    near_send(2)
-    for i in range(3):
-        sacc[i * LANES : (i + 1) * LANES, :] = rows_of(student_scale[:, i * LANES : (i + 1) * LANES])
-    near_wait(2)
-    far_send(2)
-    unpack(1.0 / (PROTOS * far_wait(2)))
-    row_pass()
-    for i in range(3):
-        pm[1, p, 0:1, i * LANES : (i + 1) * LANES] = lanes_of(acc, i)
-    group_send(pm.at[1], 2)
-    rowg[...] = jnp.zeros_like(rowg)
-    set_u((gain * CROPS) * crop_scale(group_wait(pm.at[1], 2)))
+    await_bytes(zbs.at[pl.ds(0, 7)], zb_r.at[3])
+    await_bytes(zbs.at[pl.ds(0, 7)], zb_s.at[3])
+    set_u(sacc, gain / jnp.sum(zbs[...], axis=0))
+    z_wait(zb.at[1], 2)
+    set_u(ub, (gain * CROPS) * of_group(1, zh))
 
     def c_copy(i):
         cols = ds(i * CHUNK, CHUNK)
@@ -398,12 +506,12 @@
     lax.fori_loop(0, NCHUNK, grad_chunk, 0)
     rs_x_send(1, rowg, rxrecv)
     lax.fori_loop(0, NCHUNK, column_chunk, 0)
-    pack(3)
-    near_send(3)
+    pack(1)
+    near_send(1)
     rs_z_send(1, rowg, rxrecv, rzsrc, rzrecv)
     lax.fori_loop(0, NCHUNK, y_sends, 0)
-    near_wait(3)
-    far_send(3)
+    near_wait(1)
+    far_send(1)
     lax.fori_loop(0, ZH0, zh_send, 0)
 
     @pl.when(owner)
@@ -417,9 +525,9 @@
     lax.fori_loop(ZH0, ZH1, zh_send, 0)
     ag_x_send(1, brows)
     lax.fori_loop(ZH1, NCHUNK, zh_send, 0)
-    unpack(far_wait(3))
+    unpack(far_wait(1))
     bg = ag_wait(1, brows)
-    wg = lax.dot_general(hidden[...], bg, (((0,), (0,)), ((), ())), preferred_element_type=F32)
+    wg = jnp.dot(hidden[...], bg, preferred_element_type=F32)
     wsrc[...] = wg.reshape(8, 8, DIM)
     for d in range(1, 8):
         remote(wsrc.at[(k + d) % 8], wrecv.at[k], w_s, w_r, near(d)).start()
@@ -430,7 +538,8 @@
         s = total[:, cols] + zhrecv[:, cols].astype(F32)
         sc = cscale[0:1, cols]
         un = sp[ds(b * OWN, OWN), cols].astype(F32) * sc
-        out_pg[:, cols] = sc * (s - un * vrow[0:1, cols])
+        total[:, cols] = sc * (s - un * vrow[0:1, cols])
+        pltpu.make_async_copy(total.at[:, cols], out_pg.at[:, cols], out_s.at[i]).start()
         return 0
 
     await_bytes(wrecv.at[pl.ds(0, 7)], w_r)
@@ -447,13 +556,37 @@
         remote(wfull.at[k], wfull.at[k], wg_s, wg_r, near(d)).start()
     await_bytes(wfull.at[pl.ds(0, 7)], wg_r)
     await_bytes(wfull.at[pl.ds(0, 7)], wg_s)
-    out_wg[...] = wfull[...].reshape(64, DIM)
+    last = pltpu.make_async_copy(wfull, out_wg, out_s.at[NCHUNK])
+    last.start()
+
+    def sent(i, _):
+        cols = ds(i * CHUNK, CHUNK)
+        pltpu.make_async_copy(total.at[:, cols], out_pg.at[:, cols], out_s.at[i]).wait()
+        return 0
+
+    lax.fori_loop(0, NCHUNK, sent, 0)
+    last.wait()
+
+
+def move(pg_in, wg_in, pg, wg, pg_buf, wg_buf, sem):
+    stages = [(pg_in, pg_buf, pg), (wg_in, wg_buf, wg)]
+    loads = [pltpu.make_async_copy(src, buf, sem.at[i]) for i, (src, buf, _) in enumerate(stages)]
+    stores = [pltpu.make_async_copy(buf, dst, sem.at[2 + i]) for i, (_, buf, dst) in enumerate(stages)]
+    for copy in loads:
+        copy.start()
+    for i in (1, 0):
+        loads[i].wait()
+        stores[i].start()
+    for copy in stores:
+        copy.wait()
 
 
 def per_device(hidden, w_last, student_protos, teacher_bneck, teacher_protos):
     vm = pltpu.VMEM
     dma = pltpu.SemaphoreType.DMA
     scratch = [
+        vm((64, ROWS), BF16), vm((64, DIM), BF16), vm((DIM, COLS), BF16), vm((ROWS, DIM), BF16),
+        vm((DIM, COLS), BF16), dma((8,)), dma((NCHUNK + 1,)),
         vm((ROWS, COLS), F32), vm((ROWS, COLS), F32), vm((DIM, COLS), BF16), vm((8, COLS), F32),
         vm((ROWS, DIM), BF16), vm((ROWS, LANES), F32), vm((8, COLS), F32), vm((8, COLS), F32),
         vm((ROWS, LANES), F32), vm((ROWS, LANES), F32), vm((ROWS, DIM), F32),
@@ -461,25 +594,31 @@
         vm((OWN, DIM), F32), vm((OWN, DIM), F32), vm((NX, 96, DIM), BF16), vm((ROWS, DIM), F32),
         vm((3, 96, DIM), F32), vm((SHARDS, OWN, DIM), F32), vm((NZ, OWN, DIM), F32),
         vm((NX, 96, DIM), BF16),
-        vm((4, 8, 32, LANES), F32), vm((4, 32, LANES), F32), vm((4, 32, LANES), F32),
-        vm((2, 32, 1, ROWS), F32), vm((32, 1, 2 * ROWS), F32),
+        vm((2, 8, 32, LANES), F32), vm((2, 32, LANES), F32), vm((2, 32, LANES), F32),
+        vm((2, 8, 16, LANES), F32), vm((2, 16, LANES), F32),
+        vm((NX, 1, ROWS), F32), vm((16, 1, ROWS), F32), vm((2, NX, 2, 1, ROWS), F32),
+        vm((2, 16, 2, 1, ROWS), F32), vm((NX, 1, ROWS), F32), vm((NZ, 1, ROWS), F32),
+        vm((ROWS, HALF), F32), vm((NX, 96, DIM), BF16), vm((ROWS, LANES), F32),
+        vm((ROWS, LANES), F32),
         vm((ROWS, COLS), BF16), vm((8, 2, OWN, COLS), F32), vm((8, OWN, COLS), F32), vm((NY, 2, OWN, COLS), BF16),
         vm((3, 2, OWN, COLS), BF16), vm((OWN, COLS), BF16), vm((OWN, COLS), BF16),
         vm((OWN, COLS), F32),
         vm((8, 8, DIM), F32), vm((8, 8, DIM), F32), vm((8, DIM), F32), vm((8, DIM), F32),
         vm((8, 8, DIM), F32),
-        dma((4,)), dma((4,)), dma((4,)), dma((4,)), dma((3,)), dma((3,)),
+        dma((2,)), dma((2,)), dma((2,)), dma((2,)), dma((2,)), dma((2,)), dma, dma,
+        dma((4,)), dma((4,)), dma((4,)), dma((4,)), dma, dma, dma, dma,
         dma((2,)), dma((2,)), dma((2,)), dma((2,)), dma((2,)), dma((2,)), dma((2,)), dma((2,)),
         dma((NCHUNK,)), dma((NCHUNK,)), dma((NCHUNK, 3)), dma((NCHUNK, 3)),
         dma((NCHUNK,)), dma((NCHUNK,)), dma, dma, dma, dma, dma, dma,
     ]
-    spec = pl.BlockSpec(memory_space=pltpu.VMEM)
-    return pl.pallas_call(
+    spec = pl.BlockSpec(memory_space=pl.ANY)
+    shapes = (
+        jax.ShapeDtypeStruct((OWN, COLS), F32),
+        jax.ShapeDtypeStruct((8, 8, DIM), F32),
+    )
+    results = pl.pallas_call(
         kernel,
-        out_shape=(
-            jax.ShapeDtypeStruct((OWN, COLS), F32),
-            jax.ShapeDtypeStruct((64, DIM), F32),
-        ),
+        out_shape=shapes,
         in_specs=[spec] * 5,
         out_specs=(spec, spec),
         scratch_shapes=scratch,
@@ -487,7 +626,16 @@
             collective_id=0, has_side_effects=True, vmem_limit_bytes=60 * 1024 * 1024
         ),
         name="dino_head",
-    )(hidden, w_last, student_protos, teacher_bneck, teacher_protos)
+    )(hidden.T, w_last, student_protos, teacher_bneck, teacher_protos)
+    proto_grad, weight_grad = pl.pallas_call(
+        move,
+        out_shape=shapes,
+        in_specs=[spec] * 2,
+        out_specs=(spec, spec),
+        scratch_shapes=[vm((OWN, COLS), F32), vm((8, 8, DIM), F32), dma((4,))],
+        name="move_results",
+    )(*results)
+    return proto_grad, weight_grad.reshape(64, DIM)
 
 
 def solution(mesh):

time: 135 us -> 127 us (0.941); the launches traced: 135 us -> 125 us
  Pallas kernels: 130 us -> 125 us
  local copies, waits for them, and re-layouts: 4.69 us -> 0 us
    pallas_call x1 -> x2, Pallas kernels: 130 us -> 125 us  [the longest x1 123 us: per_device(): pl.pallas_call(kernel, out_shape=shapes, in_specs=[spec] * 5, out_specs=(...]
    unnamed x3 -> x0, local copies, waits for them, and re-layouts: 4.69 us -> none
where the time goes in v3:
time: 127 us; the launch traced here: 125 us
  Pallas kernels  125 us (98%)
    pallas_call x1, Pallas kernels, per_device(): pl.pallas_call(kernel, out_shape=shapes, in_specs=[spec] * 5, out_specs=(...  123 us

profile of v3, /device:TPU:1, one launch (start us, length us, event | category | flops | bytes accessed | tf_op | source)
XLA Modules:
  0.0 125.2 jit_solution(8872700832628917288)
XLA Ops:
  0.6 122.9 %dino_head.1 = (f32[16,4096]{1,0:T(8,128)}, f32[8,8,256]{2,1,0:T(8,128)}) custom-call(bf16[64,384]{1,0:T(8,128)(2,1)} %bitcast.2, bf16[64,256]{1,0:T(8,128)(2,1)} %w_in.1, bf16[256,4096]{1,0:T(8,128)(2,1)} %sp_in.1, bf16[384,256]{1,0:T(8,128)(2,1)} %tb_in.1, bf16[256,4096]{1,0:T(8,128)(2,1)} %tp_in.1), custom_call_target="tpu_custom_call" | custom-call | tf_op jit(solution)/shard_map/dino_head/pallas_call | solution.py:619
  123.5 1.7 %move_results.1 = (f32[16,4096]{1,0:T(8,128)}, f32[8,8,256]{2,1,0:T(8,128)}) custom-call(f32[16,4096]{1,0:T(8,128)} %get-tuple-element.6.pg_in, f32[8,8,256]{2,1,0:T(8,128)} %get-tuple-element.7.wg_in), custom_call_target="tpu_custom_call" | custom-call | tf_op jit(solution)/shard_map/move_results/pallas_call | solution.py:630

commit v4 on v3

--- a/solution.py
+++ b/solution.py
@@ -24,7 +24,6 @@
 HALF = COLS // 2
 LANES = 128
 NX, NZ, NY = 4, 8, 4
-ZH0, ZH1 = 0, 4
 OWN = 16
 SHARDS = 6
 
@@ -242,63 +241,67 @@
             vrow[0:1, ds(half0 + j * LANES, LANES)] = v[j : j + 1, :]
         return v
 
-    def rs_x_send(s, src, dst):
+    def rs_x_send(s, half, src, dst):
         for d in range(1, NX):
-            rows = ds(((x + d) % NX) * 96, 96)
-            remote(src.at[rows], dst.at[d - 1], x_s.at[s], x_r.at[s], along_x(d)).start()
-
-    def rs_z_send(s, src, xr, zs, zr):
-        await_bytes(xr, x_r.at[s])
-        red = src[ds(x * 96, 96), :] + xr[0] + xr[1] + xr[2]
-        zs[...] = red.reshape(SHARDS, OWN, DIM)
+            rows = ds(half * 192 + ((x + d) % NX) * 48, 48)
+            remote(
+                src.at[rows], dst.at[half, d - 1], x_s.at[s, half], x_r.at[s, half], along_x(d)
+            ).start()
+
+    def rs_z_send(s, half, src, xr, zs, zr):
+        await_bytes(xr.at[half], x_r.at[s, half])
+        red = src[ds(half * 192 + x * 48, 48), :] + xr[half, 0] + xr[half, 1] + xr[half, 2]
+        zs[half] = red.reshape(3, OWN, DIM)
+        for jj in range(3):
+            to = 2 * jj + half + 1
+
+            @pl.when(z != to)
+            def _():
+                remote(zs.at[half, jj], zr.at[z], z_s.at[s], z_r.at[s], at_z(to)).start()
+
+    owner = jnp.logical_and(z >= 1, z <= SHARDS)
+    my_half = (z - 1) % 2
+    my_rows = ds((z - 1) // 2 * OWN, OWN)
+
+    def rs_z_wait(s, zs, zr):
+        await_bytes(zr.at[pl.ds(0, 7)], z_r.at[s])
+        zr[z] = zs[my_half, (z - 1) // 2]
+        return jnp.sum(zr[...], axis=0)
+
+    def rs_sent(s, xr, zr):
+        for half in range(2):
+            await_bytes(xr.at[half], x_s.at[s, half])
+
+        @pl.when(owner)
+        def _():
+            await_bytes(zr.at[pl.ds(0, SHARDS - 1)], z_s.at[s])
+
+        @pl.when(jnp.logical_not(owner))
+        def _():
+            await_bytes(zr.at[pl.ds(0, SHARDS)], z_s.at[s])
+
+    def ag_z_send(s, full):
+        ref = full.at[my_half, x, my_rows]
+        for d in range(1, NZ):
+            remote(ref, ref, az_s.at[s], az_r.at[s, z - 1], at_z((z + d) % NZ)).start()
+
+    def ag_x_send(s, full):
         for j in range(SHARDS):
             @pl.when(z != j + 1)
             def _():
-                remote(zs.at[j], zr.at[z], z_s.at[s], z_r.at[s], at_z(j + 1)).start()
-
-    owner = jnp.logical_and(z >= 1, z <= SHARDS)
-
-    def rs_z_wait(s, zs, zr):
-        await_bytes(zr.at[pl.ds(0, 7)], z_r.at[s])
-        zr[z] = zs[z - 1]
-        return jnp.sum(zr[...], axis=0)
-
-    def rs_sent(s, xr, zs):
-        await_bytes(xr, x_s.at[s])
-
-        @pl.when(owner)
-        def _():
-            await_bytes(zs.at[pl.ds(0, SHARDS - 1)], z_s.at[s])
-
-        @pl.when(jnp.logical_not(owner))
-        def _():
-            await_bytes(zs, z_s.at[s])
-
-    def ag_z_send(s, full):
-        ref = full.at[x, ds((z - 1) * OWN, OWN)]
-        for d in range(1, NZ):
-            remote(ref, ref, az_s.at[s], az_r.at[s], at_z((z + d) % NZ)).start()
-
-    def ag_x_send(s, full):
-        @pl.when(owner)
-        def _():
-            await_bytes(full.at[0, pl.ds(0, (SHARDS - 1) * OWN)], az_r.at[s])
-
-        @pl.when(jnp.logical_not(owner))
-        def _():
-            await_bytes(full.at[0], az_r.at[s])
+                await_bytes(full.at[j % 2, x, pl.ds(j // 2 * OWN, OWN)], az_r.at[s, j])
 
         for d in range(1, NX):
-            remote(full.at[x], full.at[x], ax_s.at[s], ax_r.at[s], along_x(d)).start()
+            remote(full.at[:, x], full.at[:, x], ax_s.at[s], ax_r.at[s], along_x(d)).start()
 
     def ag_wait(s, full):
-        await_bytes(full.at[pl.ds(0, 3)], ax_r.at[s])
-        await_bytes(full.at[pl.ds(0, 3)], ax_s.at[s])
+        await_bytes(full.at[:, pl.ds(0, 3)], ax_r.at[s])
+        await_bytes(full.at[:, pl.ds(0, 3)], ax_s.at[s])
 
         @pl.when(owner)
         def _():
             for d in range(1, NZ):
-                await_bytes(full.at[0, pl.ds(0, OWN)], az_s.at[s])
+                await_bytes(full.at[0, 0, pl.ds(0, OWN)], az_s.at[s])
 
         return full[...].reshape(ROWS, DIM)
 
@@ -308,7 +311,8 @@
     part[...] = lax.dot_general(
         hidden[...], w_last[...], (((0,), (0,)), ((), ())), preferred_element_type=F32
     )
-    rs_x_send(0, part, xrecv)
+    rs_x_send(0, 0, part, xrecv)
+    rs_x_send(0, 1, part, xrecv)
     loads[3].wait()
 
     def student_cols(i, _):
@@ -334,7 +338,8 @@
     for d in range(1, NX):
         remote(tpr.at[x], tpr.at[x], tx_s, tx_r, along_x(d)).start()
     z_send(zb1, 0, x_wait(xb1, 0))
-    rs_z_send(0, part, xrecv, zsrc, zrecv)
+    rs_z_send(0, 0, part, xrecv, zsrc, zrecv)
+    rs_z_send(0, 1, part, xrecv, zsrc, zrecv)
     await_bytes(tpr.at[pl.ds(0, 3)], tx_r)
     await_bytes(tpr.at[pl.ds(0, 3)], tx_s)
 
@@ -371,11 +376,11 @@
         u = bott * sc
         unit[...] = u
         rscale[...] = jnp.broadcast_to(sc, (OWN, DIM))
-        srows[x, ds((z - 1) * OWN, OWN), :] = u.astype(BF16)
+        srows[my_half, x, my_rows, :] = u.astype(BF16)
         ag_z_send(0, srows)
 
     z_send(zb.at[0], 1, x_wait(xb.at[0], 1))
-    rs_sent(0, xrecv, zsrc)
+    rs_sent(0, xrecv, zrecv)
     ag_x_send(0, srows)
     z_wait(zb.at[0], 1)
 
@@ -409,7 +414,10 @@
     for i in range(3):
         xbs[x, 0:1, i * LANES : (i + 1) * LANES] = lanes_of(sacc, i)
     x_send(xbs, 3)
-    z_send(zb.at[1], 2, x_wait(xb.at[1], 2))
+    zb[1, gz] = x_wait(xb.at[1], 2)
+    for d in range(1, 16):
+        part_ref = zb.at[1, gz, (gz + d) % 16 // NZ]
+        remote(part_ref, part_ref, zb_s.at[2], zb_r.at[2], ring(d)).start()
     zbs[z] = x_wait(xbs, 3)
     for d in range(1, NZ):
         remote(zbs.at[z], zbs.at[z], zb_s.at[3], zb_r.at[3], at_z((z + d) % NZ)).start()
@@ -423,7 +431,8 @@
     await_bytes(zbs.at[pl.ds(0, 7)], zb_r.at[3])
     await_bytes(zbs.at[pl.ds(0, 7)], zb_s.at[3])
     set_u(sacc, gain / jnp.sum(zbs[...], axis=0))
-    z_wait(zb.at[1], 2)
+    await_bytes(zb.at[1, pl.ds(0, 15), zh], zb_r.at[2])
+    await_bytes(zb.at[1, pl.ds(0, 15), zh], zb_s.at[2])
     set_u(ub, (gain * CROPS) * of_group(1, zh))
 
     def c_copy(i):
@@ -470,22 +479,25 @@
         zh_copy(i).start()
         return 0
 
-    def grad_chunk(i, _):
-        cols = ds(i * CHUNK, CHUNK)
-        v = vrow[0:1, cols]
-        pieces = []
-        for j in range(CHUNK // LANES):
-            lane = ds(i * CHUNK + j * LANES, LANES)
-            vj = v[:, j * LANES : (j + 1) * LANES]
-            pieces.append(
-                (sexp[:, lane] * sacc[...] - (kexp[:, lane] * vj) * ub[...]).astype(BF16)
+    def grad_half(half):
+        rows = slice(half * 192, half * 192 + 192)
+
+        def step(i, _):
+            cols = ds(i * WIDE, WIDE)
+            pieces = []
+            for j in range(WIDE // LANES):
+                lane = ds(i * WIDE + j * LANES, LANES)
+                targets = (kexp[rows, lane] * vrow[0:1, lane]) * ub[rows, :]
+                pieces.append((sexp[rows, lane] * sacc[rows, :] - targets).astype(BF16))
+            lg = jnp.concatenate(pieces, axis=1)
+            lgs[rows, cols] = lg
+            rowg[rows, :] += lax.dot_general(
+                lg, scols[:, cols], (((1,), (1,)), ((), ())), preferred_element_type=F32
             )
-        lg = jnp.concatenate(pieces, axis=1)
-        lgs[:, cols] = lg
-        rowg[...] += lax.dot_general(
-            lg, scols[:, cols], (((1,), (1,)), ((), ())), preferred_element_type=F32
-        )
-        return 0
+            return 0
+
+        lax.fori_loop(0, COLS // WIDE, step, 0)
+        rs_x_send(1, half, rowg, rxrecv)
 
     def column_chunk(i, _):
         cols = ds(i * CHUNK, CHUNK)
@@ -503,28 +515,27 @@
         y_send(i)
         return 0
 
-    lax.fori_loop(0, NCHUNK, grad_chunk, 0)
-    rs_x_send(1, rowg, rxrecv)
+    grad_half(0)
+    grad_half(1)
     lax.fori_loop(0, NCHUNK, column_chunk, 0)
     pack(1)
     near_send(1)
-    rs_z_send(1, rowg, rxrecv, rzsrc, rzrecv)
+    rs_z_send(1, 0, rowg, rxrecv, rzsrc, rzrecv)
+    rs_z_send(1, 1, rowg, rxrecv, rzsrc, rzrecv)
     lax.fori_loop(0, NCHUNK, y_sends, 0)
     near_wait(1)
     far_send(1)
-    lax.fori_loop(0, ZH0, zh_send, 0)
 
     @pl.when(owner)
     def _():
         g = rs_z_wait(1, rzsrc, rzrecv)
         u = unit[...]
         dot = jnp.sum(u * g, axis=1, keepdims=True)
-        brows[x, ds((z - 1) * OWN, OWN), :] = (rscale[...] * (g - u * dot)).astype(BF16)
+        brows[my_half, x, my_rows, :] = (rscale[...] * (g - u * dot)).astype(BF16)
         ag_z_send(1, brows)
 
-    lax.fori_loop(ZH0, ZH1, zh_send, 0)
     ag_x_send(1, brows)
-    lax.fori_loop(ZH1, NCHUNK, zh_send, 0)
+    lax.fori_loop(0, NCHUNK, zh_send, 0)
     unpack(far_wait(1))
     bg = ag_wait(1, brows)
     wg = jnp.dot(hidden[...], bg, preferred_element_type=F32)
@@ -548,7 +559,7 @@
     wf = remote(wfsrc, wfrecv, wf_s, wf_r, far())
     wf.start()
     lax.fori_loop(0, NCHUNK, finish, 0)
-    rs_sent(1, rxrecv, rzsrc)
+    rs_sent(1, rxrecv, rzrecv)
     await_bytes(wsrc.at[pl.ds(0, 7)], w_s)
     wf.wait()
     wfull[k] = wfsrc[...] + wfrecv[...]
@@ -590,10 +601,10 @@
         vm((ROWS, COLS), F32), vm((ROWS, COLS), F32), vm((DIM, COLS), BF16), vm((8, COLS), F32),
         vm((ROWS, DIM), BF16), vm((ROWS, LANES), F32), vm((8, COLS), F32), vm((8, COLS), F32),
         vm((ROWS, LANES), F32), vm((ROWS, LANES), F32), vm((ROWS, DIM), F32),
-        vm((3, 96, DIM), F32), vm((SHARDS, OWN, DIM), F32), vm((NZ, OWN, DIM), F32),
-        vm((OWN, DIM), F32), vm((OWN, DIM), F32), vm((NX, 96, DIM), BF16), vm((ROWS, DIM), F32),
-        vm((3, 96, DIM), F32), vm((SHARDS, OWN, DIM), F32), vm((NZ, OWN, DIM), F32),
-        vm((NX, 96, DIM), BF16),
+        vm((2, 3, 48, DIM), F32), vm((2, 3, OWN, DIM), F32), vm((NZ, OWN, DIM), F32),
+        vm((OWN, DIM), F32), vm((OWN, DIM), F32), vm((2, NX, 48, DIM), BF16), vm((ROWS, DIM), F32),
+        vm((2, 3, 48, DIM), F32), vm((2, 3, OWN, DIM), F32), vm((NZ, OWN, DIM), F32),
+        vm((2, NX, 48, DIM), BF16),
         vm((2, 8, 32, LANES), F32), vm((2, 32, LANES), F32), vm((2, 32, LANES), F32),
         vm((2, 8, 16, LANES), F32), vm((2, 16, LANES), F32),
         vm((NX, 1, ROWS), F32), vm((16, 1, ROWS), F32), vm((2, NX, 2, 1, ROWS), F32),
@@ -607,7 +618,7 @@
         vm((8, 8, DIM), F32),
         dma((2,)), dma((2,)), dma((2,)), dma((2,)), dma((2,)), dma((2,)), dma, dma,
         dma((4,)), dma((4,)), dma((4,)), dma((4,)), dma, dma, dma, dma,
-        dma((2,)), dma((2,)), dma((2,)), dma((2,)), dma((2,)), dma((2,)), dma((2,)), dma((2,)),
+        dma((2, 2)), dma((2, 2)), dma((2,)), dma((2,)), dma((2,)), dma((2, SHARDS)), dma((2,)), dma((2,)),
         dma((NCHUNK,)), dma((NCHUNK,)), dma((NCHUNK, 3)), dma((NCHUNK, 3)),
         dma((NCHUNK,)), dma((NCHUNK,)), dma, dma, dma, dma, dma, dma,
     ]

time: 127 us -> 124 us (0.976); the launches traced: 125 us -> 124 us
  Pallas kernels: 125 us -> 123 us
    pallas_call x1, Pallas kernels: 123 us -> 121 us  [per_device(): pl.pallas_call(kernel, out_shape=shapes, in_specs=[spec] * 5, out_specs=(...]
where the time goes in v4:
time: 124 us
  Pallas kernels  123 us (99%)
    pallas_call x1, Pallas kernels, per_device(): pl.pallas_call(kernel, out_shape=shapes, in_specs=[spec] * 5, out_specs=(...  121 us

profile of v4, /device:TPU:1, one launch (start us, length us, event | category | flops | bytes accessed | tf_op | source)
XLA Modules:
  0.0 123.7 jit_solution(8541777629182171786)
XLA Ops:
  0.6 121.4 %dino_head.1 = (f32[16,4096]{1,0:T(8,128)}, f32[8,8,256]{2,1,0:T(8,128)}) custom-call(bf16[64,384]{1,0:T(8,128)(2,1)} %bitcast.2, bf16[64,256]{1,0:T(8,128)(2,1)} %w_in.1, bf16[256,4096]{1,0:T(8,128)(2,1)} %sp_in.1, bf16[384,256]{1,0:T(8,128)(2,1)} %tb_in.1, bf16[256,4096]{1,0:T(8,128)(2,1)} %tp_in.1), custom_call_target="tpu_custom_call" | custom-call | tf_op jit(solution)/shard_map/dino_head/pallas_call | solution.py:630
  122.0 1.7 %move_results.1 = (f32[16,4096]{1,0:T(8,128)}, f32[8,8,256]{2,1,0:T(8,128)}) custom-call(f32[16,4096]{1,0:T(8,128)} %get-tuple-element.6.pg_in, f32[8,8,256]{2,1,0:T(8,128)} %get-tuple-element.7.wg_in), custom_call_target="tpu_custom_call" | custom-call | tf_op jit(solution)/shard_map/move_results/pallas_call | solution.py:641

commit v5 on v4

--- a/solution.py
+++ b/solution.py
@@ -210,22 +210,17 @@
 
     def half_cols(s):
         def step(i, _):
-            def rows_step(r, sums):
-                for q in range(2):
-                    rows = ds(r * 16 + q * 8, 8)
-                    f = ub[rows, :]
-                    g = ubp[rows, :]
-                    sums = tuple(
-                        sums[j]
-                        + kexp[rows, ds(half0 + i * WIDE + j * LANES, LANES)] * f
-                        + kp[rows, ds(i * WIDE + j * LANES, LANES)] * g
-                        for j in range(8)
-                    )
-                return sums
-
-            zero = jnp.zeros((8, LANES), F32)
-            sums = lax.fori_loop(0, ROWS // 16, rows_step, (zero,) * 8)
-            sums = [jnp.sum(v, axis=0, keepdims=True) for v in sums]
+            sums = []
+            for j in range(0, 8, 4):
+                own = [ds(half0 + i * WIDE + (j + q) * LANES, LANES) for q in range(4)]
+                other = [ds(i * WIDE + (j + q) * LANES, LANES) for q in range(4)]
+                a = [jnp.zeros((8, LANES), F32)] * 4
+                for r in range(0, ROWS, 8):
+                    f = ub[r : r + 8, :]
+                    g = ubp[r : r + 8, :]
+                    for q in range(4):
+                        a[q] = a[q] + kexp[r : r + 8, own[q]] * f + kp[r : r + 8, other[q]] * g
+                sums += [jnp.sum(v, axis=0, keepdims=True) for v in a]
             nbh[s, k, ds(i * 8, 8), :] = jnp.concatenate(sums, axis=0)
             return 0
 

time: 124 us -> 119 us (0.960)
  Pallas kernels: 123 us -> 119 us
    pallas_call x1, Pallas kernels: 121 us -> 117 us  [per_device(): pl.pallas_call(kernel, out_shape=shapes, in_specs=[spec] * 5, out_specs=(...]
where the time goes in v5:
time: 119 us
  Pallas kernels  119 us (100%)
    pallas_call x1, Pallas kernels, per_device(): pl.pallas_call(kernel, out_shape=shapes, in_specs=[spec] * 5, out_specs=(...  117 us

profile of v5, /device:TPU:1, one launch (start us, length us, event | category | flops | bytes accessed | tf_op | source)
XLA Modules:
  0.0 119.3 jit_solution(1546389675915113636)
XLA Ops:
  0.6 117.0 %dino_head.1 = (f32[16,4096]{1,0:T(8,128)}, f32[8,8,256]{2,1,0:T(8,128)}) custom-call(bf16[64,384]{1,0:T(8,128)(2,1)} %bitcast.2, bf16[64,256]{1,0:T(8,128)(2,1)} %w_in.1, bf16[256,4096]{1,0:T(8,128)(2,1)} %sp_in.1, bf16[384,256]{1,0:T(8,128)(2,1)} %tb_in.1, bf16[256,4096]{1,0:T(8,128)(2,1)} %tp_in.1), custom_call_target="tpu_custom_call" | custom-call | tf_op jit(solution)/shard_map/dino_head/pallas_call | solution.py:625
  117.6 1.7 %move_results.1 = (f32[16,4096]{1,0:T(8,128)}, f32[8,8,256]{2,1,0:T(8,128)}) custom-call(f32[16,4096]{1,0:T(8,128)} %get-tuple-element.6.pg_in, f32[8,8,256]{2,1,0:T(8,128)} %get-tuple-element.7.wg_in), custom_call_target="tpu_custom_call" | custom-call | tf_op jit(solution)/shard_map/move_results/pallas_call | solution.py:636

commit v6 on v5

--- a/solution.py
+++ b/solution.py
@@ -188,13 +188,11 @@
         def block(r, _):
             rows = ds(r * 64, 64)
 
-            def step(i, a):
-                q = src[rows, ds(col0 + i * CHUNK, CHUNK)] * vrow[0:1, ds(v0 + i * CHUNK, CHUNK)]
-                for j in range(CHUNK // LANES):
-                    a = a + q[:, j * LANES : (j + 1) * LANES]
-                return a
-
-            dst[rows, :] = lax.fori_loop(0, chunks, step, jnp.zeros((64, LANES), F32))
+            a = jnp.zeros((64, LANES), F32)
+            for j in range(chunks * CHUNK // LANES):
+                at = j * LANES
+                a = a + src[rows, ds(col0 + at, LANES)] * vrow[0:1, ds(v0 + at, LANES)]
+            dst[rows, :] = a
             return 0
 
         lax.fori_loop(0, ROWS // 64, block, 0)

time: 119 us -> 120 us (level)
  no operation moved by 1% of the time
where the time goes in v6:
time: 120 us
  Pallas kernels  119 us (99%)
    pallas_call x1, Pallas kernels, per_device(): pl.pallas_call(kernel, out_shape=shapes, in_specs=[spec] * 5, out_specs=(...  118 us

profile of v6, /device:TPU:1, one launch (start us, length us, event | category | flops | bytes accessed | tf_op | source)
XLA Modules:
  0.0 119.9 jit_solution(4346539421179360008)
XLA Ops:
  0.6 117.6 %dino_head.1 = (f32[16,4096]{1,0:T(8,128)}, f32[8,8,256]{2,1,0:T(8,128)}) custom-call(bf16[64,384]{1,0:T(8,128)(2,1)} %bitcast.2, bf16[64,256]{1,0:T(8,128)(2,1)} %w_in.1, bf16[256,4096]{1,0:T(8,128)(2,1)} %sp_in.1, bf16[384,256]{1,0:T(8,128)(2,1)} %tb_in.1, bf16[256,4096]{1,0:T(8,128)(2,1)} %tp_in.1), custom_call_target="tpu_custom_call" | custom-call | tf_op jit(solution)/shard_map/dino_head/pallas_call | solution.py:623
  118.3 1.7 %move_results.1 = (f32[16,4096]{1,0:T(8,128)}, f32[8,8,256]{2,1,0:T(8,128)}) custom-call(f32[16,4096]{1,0:T(8,128)} %get-tuple-element.6.pg_in, f32[8,8,256]{2,1,0:T(8,128)} %get-tuple-element.7.wg_in), custom_call_target="tpu_custom_call" | custom-call | tf_op jit(solution)/shard_map/move_results/pallas_call | solution.py:634
